TPU v7x, 128 devices: a whole 4x4x4 slice. The times are simulated.
128 devices in a mesh: dp: 32 (over y, x, core), head: 4 (over z).
Axes of the slice: x: 4, y: 4, z: 4, core: 2. Of those that a mesh axis runs over, the one named last changes fastest.
Arguments:
- tile_features: bfloat16 [64, 1601, 7680], P('dp', None, 'head'), may hold values from -6 to 6
- projection: bfloat16 [7680, 8, 256], P('head'), may hold values from -0.09375 to 0.09375
- queries: bfloat16 [32, 64, 8192], P('dp', None, 'head'), may hold values from -36 to 36
- query_gain: float32 [128], replicated, may hold values from 1 to 2.2
- key_gain: float32 [128], replicated, may hold values from 1 to 2.2
- tile_count: int32 [32], P('dp'), may hold values from 1 to 4, as said below
- tile_slot: int32 [32, 4], P('dp'), may hold values from 0 to 63, as said below
- cross_mask: int32 [32, 64, 4], P('dp'), may hold values 0 or 1
- prompt_length: int32 [32], P('dp'), may hold values from 16 to 64, as said below
Outputs:
- context: bfloat16 [32, 64, 8192], P('dp', None, 'head')
Inputs may be any that keep to these rules, and one draw needn't show every extreme that they name: `tile_count`: the counts of each aligned group of 4 requests sum to 8; some request has 4 tiles and some has one. Slot s sits on index s // 2 of dp; every slot holds exactly one tile; for t < tile_count[r], tile_slot[r, t] is the slot of tile t of request r, one of the 8 slots of the aligned group of 4 indices of dp that holds request r; entries with t >= tile_count[r] are arbitrary slots. `prompt_length`: some request uses all 64 rows.
All inputs are finite; a program needn't handle non-finite values. No bound on the sum of `cross_mask` on one device may be relied on, other than what follows from the above.
Results may differ from a plain program's by a relative error of at most 0.04.
Values may be sent and summed in bfloat16 or wider, within the bound.
No kernel may reach another device: no remote copies, remote signals or barrier semaphores. Data moves between devices by JAX's collectives and lax.ppermute only.
A program may use at most 128 MiB of HBM per device.

v0:
```python
import math

import jax
import jax.numpy as jnp
from jax import lax
from jax.sharding import PartitionSpec as P

HEADS = 64
KVH = 8
HD = 128
MAXT = 4
GROUP = 4


def swapped(array, axis, distance):
    return lax.ppermute(array, axis, [(i, i ^ 1 << distance) for i in range(lax.axis_size(axis))])


def normalize_rows(values, row_gain):
    squares = jnp.mean(values * values, axis=-1, keepdims=True)
    return values * lax.rsqrt(squares + 1e-05) * row_gain


def attend_tile(query_block, tile_block, usable):
    key_tile = tile_block[..., :HD]
    value_tile = tile_block[..., HD:]
    scores = jnp.einsum(
        "kgpd,knd->kgpn", query_block, key_tile, preferred_element_type=jnp.float32
    ) * (1.0 / math.sqrt(HD))
    weights = jnp.where(usable[None, None, :, None], jnp.exp(scores), 0.0).astype(jnp.bfloat16)
    denominator = jnp.sum(weights, axis=-1, dtype=jnp.float32)
    numerator = jnp.einsum(
        "kgpn,knd->kgpd", weights, value_tile, preferred_element_type=jnp.float32
    )
    return (numerator, denominator)


def order_pair(upper_half, own_part, peer_part):
    return jnp.concatenate(
        [jnp.where(upper_half, peer_part, own_part), jnp.where(upper_half, own_part, peer_part)],
        axis=0,
    )


def local(
    tile_features,
    projection,
    queries,
    query_gain,
    key_gain,
    tile_count,
    tile_slot,
    cross_mask,
    prompt_length,
):
    slots_here, tile_rows, width_here = tile_features.shape
    key_heads = projection.shape[1] // lax.axis_size("head")
    group_size = HEADS // KVH
    prompt_rows = queries.shape[1]
    flat_rows = tile_features.reshape(slots_here * tile_rows, width_here)
    summed = lax.psum_scatter(
        jnp.einsum("rw,wkc->krc", flat_rows, projection, preferred_element_type=jnp.float32).astype(
            jnp.bfloat16
        ),
        "head",
        scatter_dimension=0,
        tiled=True,
    )
    kv_tiles = summed.reshape(key_heads, slots_here, tile_rows, 2 * HD)
    keys_normed = normalize_rows(kv_tiles[..., :HD].astype(jnp.float32), key_gain).astype(
        jnp.bfloat16
    )
    prepared = jnp.concatenate([keys_normed, kv_tiles[..., HD:]], axis=-1)
    query_heads = queries[0].reshape(prompt_rows, key_heads, group_size, HD)
    query_block = normalize_rows(query_heads.astype(jnp.float32), query_gain).astype(jnp.bfloat16)
    query_block = query_block.transpose(1, 2, 0, 3)
    row_index = jnp.arange(prompt_rows, dtype=jnp.int32)
    tile_range = jnp.arange(MAXT, dtype=jnp.int32)
    own_count = tile_count[0]
    own_slots = tile_slot[0]
    own_mask = cross_mask[0]
    own_length = prompt_length[0]
    own_index = lax.axis_index("dp")
    bit_count = GROUP.bit_length() - 1
    numerator = jnp.zeros((key_heads, group_size, prompt_rows, HD), jnp.float32)
    denominator = jnp.zeros((key_heads, group_size, prompt_rows), jnp.float32)
    shared = prepared.transpose(1, 0, 2, 3)
    for bit_level in range(bit_count):
        partner = swapped(shared, "dp", bit_level)
        upper_half = own_index >> bit_level & 1 == 1
        shared = order_pair(upper_half, shared, partner)
    group_base = (own_index - own_index % GROUP) * slots_here
    for tile_pos in range(MAXT):
        tile_block = lax.dynamic_index_in_dim(
            shared, own_slots[tile_pos] - group_base, 0, keepdims=False
        )
        usable = (own_mask[:, tile_pos] == 1) & (tile_pos < own_count) & (row_index < own_length)
        numer_tile, denom_tile = attend_tile(query_block, tile_block, usable)
        numerator = numerator + numer_tile
        denominator = denominator + denom_tile
    live_rows = (row_index < own_length) & jnp.any(
        (own_mask == 1) & (tile_range[None, :] < own_count), axis=1
    )
    divisor = jnp.where(live_rows[None, None, :], denominator, 1.0)
    result = jnp.where(live_rows[None, None, :, None], numerator / divisor[..., None], 0.0)
    context = result.transpose(2, 0, 1, 3).reshape(1, prompt_rows, key_heads * group_size * HD)
    return context.astype(jnp.bfloat16)


def solution(mesh):
    in_specs = (
        P("dp", None, "head"),
        P("head", None, None),
        P("dp", None, "head"),
        P(),
        P(),
        P("dp"),
        P("dp", None),
        P("dp", None, None),
        P("dp"),
    )
    out_specs = P("dp", None, "head")
    return jax.shard_map(local, mesh=mesh, in_specs=in_specs, out_specs=out_specs, check_vma=False)
```

profile of v0, /device:TPU:1, one launch (start us, length us, event | category | flops | bytes accessed | tf_op | source)
XLA Modules:
  0.0 421.5 jit_solution(5321819843994135672)
XLA Ops:
  6.5 0.0 reduce-scatter.2.cloned.1.call-start
  6.5 11.9 %copy.31 = bf16[2,1601,1920]{2,1,0:T(8,128)(2,1)} copy(bf16[2,1601,1920]{2,0,1:T(2,128)(2,1)} %param.9) | data formatting | bytes 24591360 | tf_op args[0]
  18.4 11.3 %reshape.134 = bf16[3202,1920,1]{1,0,2:T(8,128)(2,1)} reshape(bf16[2,1601,1920]{2,1,0:T(8,128)(2,1)} %copy.31) | data formatting | bytes 24591360 | tf_op jit(solution)/shard_map/reshape | solution.py:60
  29.7 34.6 %convert_bitcast_fusion = bf16[8,3202,256]{2,1,0:T(8,128)(2,1)} fusion(bf16[3202,1920,1]{1,0,2:T(8,128)(2,1)} %reshape.134, bf16[1920,8,256]{2,1,0:T(8,128)(2,1)} %param.10), kind=kOutput, calls=%fused_computation.8 | convolution fusion | flops 25188110336 | bytes 33275392 | tf_op jit(solution)/shard_map/rw,wkc->krc/dot_general | solution.py:62
  64.3 0.0 reduce-scatter.2.cloned.1.call-update
  64.3 122.8 %reduce-scatter.2.cloned.1.call-done = bf16[2,3202,256]{2,1,0:T(8,128)(2,1)} async-done(((bf16[8,3202,256]{2,1,0:T(8,128)(2,1)}), bf16[2,3202,256]{2,1,0:T(8,128)(2,1)}) %reduce-scatter.2.cloned.1.call-update) | async-done | bytes 3278864 | tf_op jit(solution)/shard_map/reduce_scatter | solution.py:61
  187.1 2.3 reshape.132
  189.4 0.0 copy-start.5
  189.4 1.0 fusion.1
  190.4 0.3 slice.77
  190.7 0.0 copy-start.1
  190.7 0.0 copy-done.5
  190.8 1.0 fusion.3
  191.8 0.0 copy-start.2
  191.8 0.4 maximum_bitcast_fusion
  192.2 0.0 copy-done.1
  192.2 18.0 %copy.33 = bf16[2,2,1601,256]{3,1,2,0:T(2,128)(2,1)S(1)} copy(bf16[2,2,1601,256]{3,2,0,1:T(8,128)(2,1)S(1)} %maximum_bitcast_fusion) | data formatting | bytes 6557696 | tf_op jit(solution)/shard_map/transpose | solution.py:87
  210.2 0.9 collective-permute-start
  211.0 5.6 %collective-permute-done = bf16[2,2,1601,256]{3,1,2,0:T(2,128)(2,1)} collective-permute-done((bf16[2,2,1601,256]{3,1,2,0:T(2,128)(2,1)S(1)}, bf16[2,2,1601,256]{3,1,2,0:T(2,128)(2,1)}, u32[]{:S(2)}, u32[]{:S(2)}) %collective-permute-start) | collective-permute-done | bytes 3278880 | tf_op jit(solution)/shard_map/ppermute | solution.py:16
  216.7 3.6 broadcast_select_fusion.3
  220.3 0.0 copy-start
  220.3 3.7 pad_maximum_fusion
  224.0 0.1 copy-done
  224.1 26.9 %copy.36 = bf16[4,2,1601,256]{3,0,2,1:T(4,128)(2,1)} copy(bf16[4,2,1601,256]{3,2,0,1:T(8,128)(2,1)} %pad_maximum_fusion) | data formatting | bytes 13115392 | tf_op jit(solution)/shard_map/concatenate | solution.py:39
  251.0 1.2 collective-permute-start.1
  252.2 1.4 fusion.23
  257.4 0.0 copy-done.4
  257.4 0.1 copy.52
  257.5 0.8 copy-done.3
  258.3 0.3 multiply_reduce_fusion
  258.6 0.1 copy.29
  258.7 0.1 copy.30
  258.8 0.8 and_reduce_fusion
  259.6 0.8 bitcast_and_fusion
  260.5 1.2 fusion.17
  261.7 132.0 %collective-permute-done.1 = bf16[4,2,1601,256]{3,0,2,1:T(4,128)(2,1)} collective-permute-done((bf16[4,2,1601,256]{3,0,2,1:T(4,128)(2,1)}, bf16[4,2,1601,256]{3,0,2,1:T(4,128)(2,1)}, u32[]{:S(2)}, u32[]{:S(2)}) %collective-permute-start.1) | collective-permute-done | bytes 6557728 | tf_op jit(solution)/shard_map/ppermute | solution.py:16
  393.8 6.0 %broadcast_select_fusion.1 = (bf16[4,2,1601,256]{3,2,0,1:T(8,128)(2,1)S(1)}, bf16[4,2,1601,256]{3,2,0,1:T(8,128)(2,1)S(1)}) fusion(pred[]{:T(512)S(6)} %eq.49, bf16[4,2,1601,256]{3,0,2,1:T(4,128)(2,1)} %collective-permute-done.1, bf16[2,2,1601,256]{3,2,0,1:T(8,128)(2,1)} %copy-done, bf16[2,2,1601,256]{3,2,0,1:T(8,128)(2,1)S(1)} %get-tuple-element.11), kind=kLoop, calls=%fused_computation.20 | loop fusion | flops 9836544 | bytes 26230784 | tf_op jit(solution)/shard_map/jit(_where)/select_n | solution.py:40
  399.8 2.7 fusion.11
  402.4 1.7 convert_reduce_fusion.2
  404.2 1.0 fusion.16
  405.2 1.8 convert_reduce_fusion
  407.0 1.7 convert_reduce_fusion.1
  408.7 1.8 convert_reduce_fusion.3
  410.5 1.0 convolution_add_fusion.2
  411.5 1.0 convolution_add_fusion.1
  412.6 1.0 fusion.15
  413.6 0.2 copy.43
  413.8 0.8 convert_element_type.79
  (8 shorter events, 0.1 us)
Async XLA Ops:
  6.5 180.6 %reduce-scatter.2.cloned.1.call-start = ((), (), s32[]{:S(2)}) async-start(), calls=%async_computation.1 | async-start | bytes 16424960 | tf_op jit(solution)/shard_map/reduce_scatter | solution.py:61
  189.4 1.3 copy-start.5
  190.7 1.5 copy-start.1
  191.8 18.4 %copy-start.2 = (bf16[2,2,1601,128]{3,2,1,0:T(8,128)(2,1)}, bf16[2,2,1601,128]{3,2,1,0:T(8,128)(2,1)S(1)}, u32[]{:S(2)}) copy-start(bf16[2,2,1601,128]{3,2,1,0:T(8,128)(2,1)S(1)} %fusion.3) | copy-start | bytes 4918276
  210.2 6.5 %collective-permute-start = (bf16[2,2,1601,256]{3,1,2,0:T(2,128)(2,1)S(1)}, bf16[2,2,1601,256]{3,1,2,0:T(2,128)(2,1)}, u32[]{:S(2)}, u32[]{:S(2)}) collective-permute-start(bf16[2,2,1601,256]{3,1,2,0:T(2,128)(2,1)S(1)} %copy.33), channel_id=1, source_target_pairs={{0,4},{4,0},{8,12},{12,8},{16,20},{20,16},{24,28},{28,24},{32,36},... | collective-permute-start | bytes 9836552 | tf_op jit(solution)/shard_map/ppermute | solution.py:16
  220.3 3.8 copy-start
  224.1 33.3 %copy-start.4 = (bf16[1,64,2048]{2,1,0:T(8,128)(2,1)S(1)}, bf16[1,64,2048]{2,1,0:T(8,128)(2,1)}, u32[]{:S(2)}) copy-start(bf16[1,64,2048]{2,1,0:T(8,128)(2,1)} %param.11) | copy-start | bytes 786436
  251.0 142.7 %collective-permute-start.1 = (bf16[4,2,1601,256]{3,0,2,1:T(4,128)(2,1)}, bf16[4,2,1601,256]{3,0,2,1:T(4,128)(2,1)}, u32[]{:S(2)}, u32[]{:S(2)}) collective-permute-start(bf16[4,2,1601,256]{3,0,2,1:T(4,128)(2,1)} %copy.36), channel_id=1, source_target_pairs={{0,8},{4,12},{8,0},{12,4},{16,24},{20,28},{24,16},{28,20},{32,40},... | collective-permute-start | bytes 19673096 | tf_op jit(solution)/shard_map/ppermute | solution.py:16
  257.5 0.8 copy-start.3
Sparse Core Ops, SparseCore 0:
  64.4 122.6 reduce-scatter.1
where the time goes:
time: 422 us; the launch traced here: 421 us
  waiting for transfers between devices  260 us (62%)
  local copies, waits for them, and re-layouts  74.3 us (18%)
  matrix products  45.7 us (11%)
  other arithmetic  21.5 us (5%)
  between operations  17.4 us (4%)
    ppermute x2, waiting for transfers between devices, swapped(): lax.ppermute(array, axis, [(i, i ^ 1 << distance) for i in range(lax.axis...  138 us
    reduce_scatter x1, waiting for transfers between devices, local(): lax.psum_scatter(jnp.einsum('rw,wkc->krc', flat_rows, projection, preferr...  123 us
    dot_general x1, matrix products, local(): jnp.einsum('rw,wkc->krc', flat_rows, projection, preferred_element_type=j...  34.6 us
    concatenate x1, local copies, waits for them, and re-layouts, order_pair(): jnp.concatenate([jnp.where(upper_half, peer_part, own_part), jnp.where(up...  26.9 us
    transpose x1, local copies, waits for them, and re-layouts, local(): shared = prepared.transpose(1, 0, 2, 3)  18 us
    unnamed x14, local copies, waits for them, and re-layouts  12.9 us
    reshape x1, local copies, waits for them, and re-layouts, local(): flat_rows = tile_features.reshape(slots_here * tile_rows, width_here)  11.3 us
    select_n x2, other arithmetic, order_pair(): jnp.where(upper_half, peer_part, own_part)  9.62 us
  transfers between devices with their start and end apart: 3, of which 3 were waited for; matrix products, arithmetic and copies ran while one was open for 1% of the time, Pallas kernels for 0%

commit v1 on v0

v1 whole, which is shorter than its diff:
```python
import math

import jax
import jax.numpy as jnp
from jax import lax
from jax.experimental import pallas as pl
from jax.experimental.pallas import tpu as pltpu
from jax.sharding import PartitionSpec as P

KVH = 8
HD = 128
MAXT = 4
GROUP = 4
NHEAD = 4
GSIZE = 8
PROMPT = 64
QROWS = GSIZE * PROMPT
TROWS = 1601
WIDTH = 1920
TILES = 2
HEADS_HERE = 2
HALF = 808
SMALL = 280
LARGE = HALF - SMALL
UP_SMALL, UP_LARGE = 0, SMALL
DOWN_LARGE, DOWN_SMALL = TROWS - HALF, TROWS - SMALL
OVERLAP = 2 * HALF - TROWS
SENT_ROWS = QROWS + 16
F32 = jnp.float32
BF16 = jnp.bfloat16
VMEM_LIMIT = 56 * 2**20


def params():
    return pltpu.CompilerParams(vmem_limit_bytes=VMEM_LIMIT)


def cost(flops, moved, exps=0):
    return pl.CostEstimate(flops=flops, bytes_accessed=moved, transcendentals=exps)


def split_heads_kernel(w_ref, out_ref):
    out_ref[...] = jnp.transpose(w_ref[...], (1, 0, 2))


def split_heads(projection):
    depth = 480
    return pl.pallas_call(
        split_heads_kernel,
        grid=(WIDTH // depth,),
        in_specs=[pl.BlockSpec((depth, KVH, 2 * HD), lambda i: (i, 0, 0))],
        out_specs=pl.BlockSpec((KVH, depth, 2 * HD), lambda i: (0, i, 0)),
        out_shape=jax.ShapeDtypeStruct((KVH, WIDTH, 2 * HD), BF16),
        compiler_params=params(),
        cost_estimate=cost(0, 4 * WIDTH * KVH * HD * 2),
        name="split_heads",
    )(projection)


def first_partial_kernel(shard_ref, x_ref, w_ref, low_ref, high_ref, flat_ref):
    rows = x_ref.shape[0]
    flat = x_ref[...].reshape(2 * rows, WIDTH)
    flat_ref[...] = flat
    low_ref[...] = jnp.dot(flat, w_ref[0], preferred_element_type=F32).astype(BF16)
    high_ref[...] = jnp.dot(flat, w_ref[1], preferred_element_type=F32).astype(BF16)


def first_partial(shards, rows_first, weights, start, count, blocks):
    block = count // blocks
    return pl.pallas_call(
        first_partial_kernel,
        grid_spec=pltpu.PrefetchScalarGridSpec(
            num_scalar_prefetch=1,
            grid=(blocks,),
            in_specs=[
                pl.BlockSpec(
                    (pl.Element(block), pl.Element(TILES), pl.Element(WIDTH)),
                    lambda i, s: (start + i * block, 0, 0),
                ),
                pl.BlockSpec((HEADS_HERE, WIDTH, 2 * HD), lambda i, s: (s[0], 0, 0)),
            ],
            out_specs=[
                pl.BlockSpec((2 * block, 2 * HD), lambda i, s: (i, 0)),
                pl.BlockSpec((2 * block, 2 * HD), lambda i, s: (i, 0)),
                pl.BlockSpec((2 * block, WIDTH), lambda i, s: (i, 0)),
            ],
        ),
        out_shape=[
            jax.ShapeDtypeStruct((2 * count, 2 * HD), BF16),
            jax.ShapeDtypeStruct((2 * count, 2 * HD), BF16),
            jax.ShapeDtypeStruct((2 * count, WIDTH), BF16),
        ],
        compiler_params=params(),
        cost_estimate=cost(2 * 2 * count * WIDTH * 512, 2 * count * WIDTH * 4),
        name="first_partial",
    )(shards, rows_first, weights)


def later_partials_kernel(shard_ref, flat_ref, w_ref, *out_refs):
    step = pl.program_id(0)
    low = jnp.dot(flat_ref[...], w_ref[0], preferred_element_type=F32).astype(BF16)
    high = jnp.dot(flat_ref[...], w_ref[1], preferred_element_type=F32).astype(BF16)
    for at in range(NHEAD - 1):

        @pl.when(step == at)
        def _():
            out_refs[2 * at][...] = low
            out_refs[2 * at + 1][...] = high


def later_partials(shards, flat, weights):
    rows = flat.shape[0]
    outs = 2 * (NHEAD - 1)
    return pl.pallas_call(
        later_partials_kernel,
        grid_spec=pltpu.PrefetchScalarGridSpec(
            num_scalar_prefetch=1,
            grid=(NHEAD - 1,),
            in_specs=[
                pl.BlockSpec((rows, WIDTH), lambda i, s: (0, 0)),
                pl.BlockSpec((HEADS_HERE, WIDTH, 2 * HD), lambda i, s: (s[i + 1], 0, 0)),
            ],
            out_specs=[pl.BlockSpec((rows, 2 * HD), lambda i, s: (0, 0))] * outs,
        ),
        out_shape=[jax.ShapeDtypeStruct((rows, 2 * HD), BF16)] * outs,
        compiler_params=params(),
        cost_estimate=cost(3 * 2 * rows * WIDTH * 512, rows * WIDTH * 2),
        name="later_partials",
    )(shards, flat, weights)


def query_kernel(info_ref, mask_ref, q_ref, gain_ref, qn_ref, owned_ref):
    me = info_ref[GROUP, 0]
    own = lax.rem(me, GROUP)
    for tile in range(TILES):
        slot = me * TILES + tile
        asker = jnp.int32(0)
        place = jnp.int32(0)
        for request in range(GROUP):
            for at in range(MAXT):
                hit = (info_ref[request, 2 + at] == slot) & (at < info_ref[request, 0])
                asker = jnp.where(hit, request, asker)
                place = jnp.where(hit, at, place)
        length = info_ref[asker, 1]
        lane = lax.broadcasted_iota(jnp.int32, (PROMPT, MAXT), 1)
        seen = jnp.sum(jnp.where(lane == place, mask_ref[asker], 0), axis=1, keepdims=True)
        row = lax.broadcasted_iota(jnp.int32, (PROMPT, HD), 0)
        usable = (jnp.broadcast_to(seen, (PROMPT, HD)) == 1) & (row < length)
        for partner in range(GROUP):
            mine = lax.bitwise_xor(own, partner) == asker
            owned_ref[partner, tile] = jnp.where(usable & mine, 1.0, 0.0)
        for head in range(HEADS_HERE):
            for member in range(GSIZE):
                column = (head * GSIZE + member) * HD
                values = q_ref[asker, :, column : column + HD].astype(F32)
                squares = jnp.mean(values * values, axis=-1, keepdims=True)
                normed = values * lax.rsqrt(squares + 1e-05) * gain_ref[...]
                qn_ref[head, tile, member * PROMPT : (member + 1) * PROMPT, :] = normed.astype(BF16)


def prepare_queries(info, masks, queries, query_gain):
    vmem = pl.BlockSpec(memory_space=pltpu.VMEM)
    return pl.pallas_call(
        query_kernel,
        in_specs=[pl.BlockSpec(memory_space=pltpu.SMEM), vmem, vmem, vmem],
        out_specs=[vmem, vmem],
        out_shape=[
            jax.ShapeDtypeStruct((HEADS_HERE, TILES, QROWS, HD), BF16),
            jax.ShapeDtypeStruct((GROUP, TILES, PROMPT, HD), F32),
        ],
        compiler_params=params(),
        cost_estimate=cost(2**22, 2**21),
        name="prepare_queries",
    )(info, masks, queries, query_gain)


def attend(up, up_own, down, down_own, qn_ref, gain_ref, total_ref, scratch, skip, first):
    key_scr, value_scr = scratch
    for part, (got, own) in enumerate(((up, up_own), (down, down_own))):
        rows = got.shape[0] // 2
        both = (got[...].astype(F32) + own[...].astype(F32)).astype(BF16).astype(F32)
        key_scr[...] = both[:, :HD]
        value_scr[...] = both[:, HD:]
        for tile in range(TILES):
            keys = key_scr[pl.ds(tile, rows, stride=2), :]
            values = value_scr[pl.ds(tile, rows, stride=2), :]
            squares = jnp.mean(keys * keys, axis=-1, keepdims=True)
            keys = (keys * lax.rsqrt(squares + 1e-05) * gain_ref[...]).astype(BF16)
            ones = jnp.ones((rows, HD), F32)
            if part == 1 and skip:
                keep = lax.broadcasted_iota(jnp.int32, (rows, HD), 0) >= skip
                values = jnp.where(keep, values, 0.0)
                ones = jnp.where(keep, 1.0, 0.0)
            wide = jnp.concatenate([values, ones], axis=1).astype(BF16)
            scores = lax.dot_general(
                qn_ref[0, tile], keys, (((1,), (1,)), ((), ())), preferred_element_type=F32
            )
            weights = jnp.exp(scores * (1.0 / math.sqrt(HD))).astype(BF16)
            term = jnp.dot(weights, wide, preferred_element_type=F32)
            if first and part == 0:
                total_ref[tile] = term
            else:
                total_ref[tile] += term


def partial_attention(head, parts, qn, key_gain, skip):
    rows = parts[0].shape[0]

    def body(up, up_own, down, down_own, qn_ref, gain_ref, total_ref, *scratch):
        attend(up, up_own, down, down_own, qn_ref, gain_ref, total_ref, scratch, skip, True)

    return pl.pallas_call(
        body,
        grid=(1,),
        in_specs=[pl.BlockSpec((rows, 2 * HD), lambda i: (0, 0))] * 4
        + [
            pl.BlockSpec((1, TILES, QROWS, HD), lambda i: (head, 0, 0, 0)),
            pl.BlockSpec((1, HD), lambda i: (0, 0)),
        ],
        out_specs=pl.BlockSpec((TILES, QROWS, 2 * HD), lambda i: (0, 0, 0)),
        out_shape=jax.ShapeDtypeStruct((TILES, QROWS, 2 * HD), F32),
        scratch_shapes=[pltpu.VMEM((rows, HD), F32)] * 2,
        compiler_params=params(),
        cost_estimate=cost(2 * 2 * rows * QROWS * 384, rows * 2048, 2 * rows * QROWS),
        name="partial_attention",
    )(*parts, qn, key_gain)


def diagonal(shape):
    row = lax.broadcasted_iota(jnp.int32, shape, 0)
    column = lax.broadcasted_iota(jnp.int32, shape, 1)
    return jnp.where(row == column, 1.0, 0.0).astype(F32)


def closing_attention(head, parts, qn, key_gain, before, owned, skip):
    rows = parts[0].shape[0]

    def body(
        up, up_own, down, down_own, qn_ref, gain_ref, before_ref, owned_ref, kept, *rest
    ):
        sent, (total_ref, key_scr, value_scr) = rest[: GROUP - 1], rest[GROUP - 1 :]
        total_ref[...] = before_ref[...]
        scratch = (key_scr, value_scr)
        attend(up, up_own, down, down_own, qn_ref, gain_ref, total_ref, scratch, skip, False)
        eye = diagonal((HD, HD))
        for partner in range(GROUP):
            rows_of = []
            for member in range(GSIZE):
                block = slice(member * PROMPT, (member + 1) * PROMPT)
                for part in range(2):
                    lanes = slice(part * HD, (part + 1) * HD)
                    held = jnp.zeros((PROMPT, HD), F32)
                    for tile in range(TILES):
                        belongs = owned_ref[partner, tile] > 0.5
                        held += jnp.where(belongs, total_ref[tile, block, lanes], 0.0)
                    if partner == 0:
                        kept[block, lanes] = held
                    elif part == 0:
                        sent[partner - 1][block, :] = held.astype(BF16)
                    else:
                        rows_of.append(held)
            if partner == 0:
                continue
            lines = []
            for at in range(QROWS // HD):
                square = jnp.concatenate([rows_of[2 * at], rows_of[2 * at + 1]], axis=0)
                lines.append(jnp.sum(square * eye, axis=0, keepdims=True))
            lines = jnp.concatenate(lines, axis=0)
            coarse = lines.astype(BF16).astype(F32)
            tail = jnp.concatenate([coarse, lines - coarse, jnp.zeros((8, HD), F32)], axis=0)
            sent[partner - 1][QROWS:, :] = tail.astype(BF16)

    whole = lambda *shape: pl.BlockSpec(shape, lambda i: (0,) * len(shape))
    return pl.pallas_call(
        body,
        grid=(1,),
        in_specs=[whole(rows, 2 * HD)] * 4
        + [
            pl.BlockSpec((1, TILES, QROWS, HD), lambda i: (head, 0, 0, 0)),
            whole(1, HD),
            whole(TILES, QROWS, 2 * HD),
            whole(GROUP, TILES, PROMPT, HD),
        ],
        out_specs=[whole(QROWS, 2 * HD)] + [whole(SENT_ROWS, HD)] * (GROUP - 1),
        out_shape=[jax.ShapeDtypeStruct((QROWS, 2 * HD), F32)]
        + [jax.ShapeDtypeStruct((SENT_ROWS, HD), BF16)] * (GROUP - 1),
        scratch_shapes=[pltpu.VMEM((TILES, QROWS, 2 * HD), F32)]
        + [pltpu.VMEM((rows, HD), F32)] * 2,
        compiler_params=params(),
        cost_estimate=cost(2 * 2 * rows * QROWS * 384, rows * 2048, 2 * rows * QROWS),
        name="closing_attention",
    )(*parts, qn, key_gain, before, owned)


def finish_kernel(info_ref, mask_ref, *refs):
    out_ref = refs[-1]
    lane = lax.broadcasted_iota(jnp.int32, (PROMPT, MAXT), 1)
    seen = jnp.where((lane < info_ref[0, 0]) & (mask_ref[0] == 1), 1, 0)
    seen = jnp.sum(seen, axis=1, keepdims=True)
    row = lax.broadcasted_iota(jnp.int32, (PROMPT, HD), 0)
    live = (jnp.broadcast_to(seen, (PROMPT, HD)) > 0) & (row < info_ref[0, 1])
    eye = diagonal((HD, HD))
    for head in range(HEADS_HERE):
        kept, *got = refs[head * GROUP : (head + 1) * GROUP]
        for at in range(QROWS // HD):
            line = jnp.zeros((1, HD), F32)
            for one in got:
                line += one[QROWS + at : QROWS + at + 1, :].astype(F32)
                line += one[QROWS + 4 + at : QROWS + 5 + at, :].astype(F32)
            square = jnp.broadcast_to(line, (HD, HD)) * eye
            spread = jnp.broadcast_to(jnp.sum(square, axis=1, keepdims=True), (HD, HD))
            block = slice(at * HD, (at + 1) * HD)
            numerator = kept[block, :HD]
            for one in got:
                numerator += one[block, :].astype(F32)
            denominator = kept[block, HD:] + spread
            for half in range(HD // PROMPT):
                inner = slice(half * PROMPT, (half + 1) * PROMPT)
                divisor = jnp.where(live, denominator[inner], 1.0)
                result = jnp.where(live, numerator[inner] / divisor, 0.0)
                column = (head * GSIZE + at * 2 + half) * HD
                out_ref[0, :, column : column + HD] = result.astype(BF16)


def finish(info, mask, parts):
    vmem = pl.BlockSpec(memory_space=pltpu.VMEM)
    return pl.pallas_call(
        finish_kernel,
        in_specs=[pl.BlockSpec(memory_space=pltpu.SMEM)] + [vmem] * (1 + len(parts)),
        out_specs=vmem,
        out_shape=jax.ShapeDtypeStruct((1, PROMPT, HEADS_HERE * GSIZE * HD), BF16),
        compiler_params=params(),
        cost_estimate=cost(2**21, 2**21),
        name="finish",
    )(info, mask, *parts)


def add(left, right):
    return (left.astype(F32) + right.astype(F32)).astype(BF16)


def local(
    tile_features,
    projection,
    queries,
    query_gain,
    key_gain,
    tile_count,
    tile_slot,
    cross_mask,
    prompt_length,
):
    here = lax.axis_index("head")
    own_index = lax.axis_index("dp")
    steps = jnp.arange(1, NHEAD + 1, dtype=jnp.int32)
    up_shards = lax.rem(here - steps + 2 * NHEAD, NHEAD)
    down_shards = lax.rem(here + steps, NHEAD)
    up_perm = [(i, (i + 1) % NHEAD) for i in range(NHEAD)]
    down_perm = [(i, (i - 1) % NHEAD) for i in range(NHEAD)]
    groups = [list(range(g, g + GROUP)) for g in range(0, lax.axis_size("dp"), GROUP)]

    weights = split_heads(projection)
    rows_first = jnp.transpose(tile_features, (1, 0, 2))
    plan = {
        "us": (up_shards, up_perm, UP_SMALL, SMALL, 1),
        "ds": (down_shards, down_perm, DOWN_SMALL, SMALL, 1),
        "ul": (up_shards, up_perm, UP_LARGE, LARGE, 2),
        "dl": (down_shards, down_perm, DOWN_LARGE, LARGE, 2),
    }
    running, flats, owned_parts = {}, {}, {}
    for name, (shards, perm, start, count, blocks) in plan.items():
        low, high, flat = first_partial(shards, rows_first, weights, start, count, blocks)
        running[name, 0], running[name, 1] = low, high
        flats[name] = flat
    for name, (shards, perm, start, count, blocks) in plan.items():
        outs = later_partials(shards, flats[name], weights)
        for at in range(NHEAD - 1):
            owned_parts[name, 0, at] = outs[2 * at]
            owned_parts[name, 1, at] = outs[2 * at + 1]
    order = [("us", 0), ("ds", 0), ("us", 1), ("ds", 1), ("ul", 0), ("dl", 0), ("ul", 1), ("dl", 1)]
    for step in range(NHEAD - 1):
        for name, head in order:
            got = lax.ppermute(running[name, head], "head", plan[name][1])
            if step < NHEAD - 2:
                got = add(got, owned_parts[name, head, step])
            running[name, head] = got

    info = jnp.concatenate([tile_count, prompt_length, tile_slot[0], jnp.zeros((2,), jnp.int32)])
    packed = jnp.concatenate([info, cross_mask.reshape(-1)])[None]
    packed_all = lax.all_gather(packed, "dp", axis=0, tiled=True, axis_index_groups=groups)
    queries_all = lax.all_gather(queries, "dp", axis=0, tiled=True, axis_index_groups=groups)
    last_line = jnp.full((1, 8), own_index, jnp.int32)
    info_all = jnp.concatenate([packed_all[:, :8], last_line], axis=0)
    masks_all = packed_all[:, 8:].reshape(GROUP, PROMPT, MAXT)
    qn, owned = prepare_queries(info_all, masks_all, queries_all, query_gain[None])

    key_line = key_gain[None]
    final = []
    last = NHEAD - 2
    for head in range(HEADS_HERE):

        def parts_of(up, down):
            return (
                running[up, head],
                owned_parts[up, head, last],
                running[down, head],
                owned_parts[down, head, last],
            )

        before = partial_attention(head, parts_of("us", "ds"), qn, key_line, 0)
        kept, *sent = closing_attention(
            head, parts_of("ul", "dl"), qn, key_line, before, owned, OVERLAP
        )
        final.append(kept)
        for partner in range(1, GROUP):
            pairs = [(i, i ^ partner) for i in range(lax.axis_size("dp"))]
            final.append(lax.ppermute(sent[partner - 1], "dp", pairs))
    return finish(info[None], cross_mask, final)


def solution(mesh):
    in_specs = (
        P("dp", None, "head"),
        P("head", None, None),
        P("dp", None, "head"),
        P(),
        P(),
        P("dp"),
        P("dp", None),
        P("dp", None, None),
        P("dp"),
    )
    out_specs = P("dp", None, "head")
    return jax.shard_map(local, mesh=mesh, in_specs=in_specs, out_specs=out_specs, check_vma=False)
```

time: 422 us -> 222 us (0.53)
  waiting for transfers between devices: 260 us -> 57.1 us
  Pallas kernels: 0 us -> 99.7 us
  local copies, waits for them, and re-layouts: 74.3 us -> 5.43 us
  matrix products: 45.7 us -> 0 us
  starting transfers between devices: 2.06 us -> 29.1 us
  other arithmetic: 21.5 us -> 4.34 us
  blocking collectives: 0 us -> 10.6 us
    reduce_scatter x1 -> x0, waiting for transfers between devices: 123 us -> none  [local(): lax.psum_scatter(jnp.einsum('rw,wkc->krc', flat_rows, projection, preferr...]
    pallas_call x0 -> x15, Pallas kernels: none -> 99.7 us  [the longest x4 42.6 us: later_partials(): pl.pallas_call(later_partials_kernel, grid_spec=pltpu.PrefetchScalarGridS...]
    ppermute x2 -> x30, waiting for transfers between devices: 138 us -> 56.4 us  [the longest x24 50.8 us: local(): got = lax.ppermute(running[name, head], 'head', plan[name][1])]
    dot_general x9 -> x0, matrix products: 45.7 us -> none  [the longest x1 34.6 us: local(): jnp.einsum('rw,wkc->krc', flat_rows, projection, preferred_element_type=j...]
    ppermute x2 -> x30, starting transfers between devices: 2.05 us -> 29.1 us  [the longest x24 21.3 us: local(): got = lax.ppermute(running[name, head], 'head', plan[name][1])]
    concatenate x1 -> x2, local copies, waits for them, and re-layouts: 26.9 us -> 0.67 us  [the longest x1 0.6 us: local(): info_all = jnp.concatenate([packed_all[:, :8], last_line], axis=0)]
    transpose x1 -> x0, local copies, waits for them, and re-layouts: 18 us -> none  [local(): shared = prepared.transpose(1, 0, 2, 3)]
    reshape x2, local copies, waits for them, and re-layouts: 13.5 us -> 0.9 us  [the longest x1 0.8 us: local(): masks_all = packed_all[:, 8:].reshape(GROUP, PROMPT, MAXT)]
  transfers between devices with their start and end apart: 3 -> 31, of which waited for: 3 -> 10; matrix products, arithmetic and copies ran while one was open for 1% -> 3% of each run, Pallas kernels for 0% -> 44%
where the time goes in v1:
time: 222 us
  Pallas kernels  99.7 us (45%)
  waiting for transfers between devices  57.1 us (26%)
  starting transfers between devices  29.1 us (13%)
  between operations  15.7 us (7%)
  blocking collectives  10.6 us (5%)
  local copies, waits for them, and re-layouts  5.43 us (2%)
  other arithmetic  4.34 us (2%)
    ppermute x24, waiting for transfers between devices, local(): got = lax.ppermute(running[name, head], 'head', plan[name][1])  50.8 us
    pallas_call x4, Pallas kernels, later_partials(): pl.pallas_call(later_partials_kernel, grid_spec=pltpu.PrefetchScalarGridS...  42.6 us
    pallas_call x4, Pallas kernels, first_partial(): pl.pallas_call(first_partial_kernel, grid_spec=pltpu.PrefetchScalarGridSp...  25.9 us
    ppermute x24, starting transfers between devices, local(): got = lax.ppermute(running[name, head], 'head', plan[name][1])  21.3 us
    pallas_call x2, Pallas kernels, closing_attention(): pl.pallas_call(body, grid=(1,), in_specs=[whole(rows, 2 * HD)] * 4 + [pl....  10.9 us
    unnamed x1, blocking collectives  10.6 us
    ppermute x6, starting transfers between devices, local(): final.append(lax.ppermute(sent[partner - 1], 'dp', pairs))  7.8 us
    pallas_call x2, Pallas kernels, partial_attention(): pl.pallas_call(body, grid=(1,), in_specs=[pl.BlockSpec((rows, 2 * HD), la...  7.77 us
  transfers between devices with their start and end apart: 31, of which 10 were waited for; matrix products, arithmetic and copies ran while one was open for 3% of the time, Pallas kernels for 44%

profile of v1, /device:TPU:1, one launch (start us, length us, event | category | flops | bytes accessed | tf_op | source)
XLA Modules:
  0.0 222.0 jit_solution(204822312346428748)
XLA Ops:
  6.5 0.7 all-gather.3.cloned.1.call-update
  7.8 7.6 %split_heads.1.w_ref = bf16[8,1920,256]{2,1,0:T(8,128)(2,1)} custom-call(bf16[1920,8,256]{2,1,0:T(8,128)(2,1)} %w_ref.1), custom_call_target="tpu_custom_call" | custom-call | bytes 15728640 | tf_op jit(solution)/shard_map/split_heads/pallas_call | solution.py:48
  15.5 5.8 %first_partial.7 = (bf16[560,256]{1,0:T(8,128)(2,1)}, bf16[560,256]{1,0:T(8,128)(2,1)}, bf16[560,1920]{1,0:T(8,128)(2,1)}) custom-call(s32[4]{0:T(128)} %get-tuple-element.97.shard_ref, bf16[1601,2,1920]{2,1,0:T(2,128)(2,1)} %bitcast.7, bf16[8,1920,256]{2,1,0:T(8,128)(2,1)} %split_heads.1.w_ref), custom_call_target="tpu_custom_call" | custom-call | flops 1101004800 | bytes 4300800 | tf_op jit(solution)/shard_map/first_partial/pallas_call | solution.py:70
  21.3 4.6 %collective-permute-start.9 = (bf16[560,256]{1,0:T(8,128)(2,1)}, bf16[560,256]{1,0:T(8,128)(2,1)S(1)}, u32[]{:S(2)}, u32[]{:S(2)}) collective-permute-start(bf16[560,256]{1,0:T(8,128)(2,1)} %get-tuple-element.67), channel_id=1, source_target_pairs={{0,3},{1,0},{2,1},{3,2},{4,7},{5,4},{6,5},{7,6},{8,11},{9,8},{10,9... | collective-permute-start | bytes 860168 | tf_op jit(solution)/shard_map/ppermute | solution.py:383
  26.0 5.9 %first_partial.6 = (bf16[560,256]{1,0:T(8,128)(2,1)}, bf16[560,256]{1,0:T(8,128)(2,1)}, bf16[560,1920]{1,0:T(8,128)(2,1)}) custom-call(s32[4]{0:T(128)} %get-tuple-element.98.shard_ref, bf16[1601,2,1920]{2,1,0:T(2,128)(2,1)} %bitcast.8, bf16[8,1920,256]{2,1,0:T(8,128)(2,1)} %split_heads.1.w_ref), custom_call_target="tpu_custom_call" | custom-call | flops 1101004800 | bytes 4300800 | tf_op jit(solution)/shard_map/first_partial/pallas_call | solution.py:70
  31.9 1.3 collective-permute-start.6
  33.3 7.1 %first_partial.5 = (bf16[1056,256]{1,0:T(8,128)(2,1)}, bf16[1056,256]{1,0:T(8,128)(2,1)}, bf16[1056,1920]{1,0:T(8,128)(2,1)}) custom-call(s32[4]{0:T(128)} %get-tuple-element.97.shard_ref, bf16[1601,2,1920]{2,1,0:T(2,128)(2,1)} %bitcast.9, bf16[8,1920,256]{2,1,0:T(8,128)(2,1)} %split_heads.1.w_ref), custom_call_target="tpu_custom_call" | custom-call | flops 2076180480 | bytes 8110080 | tf_op jit(solution)/shard_map/first_partial/pallas_call | solution.py:70
  40.3 2.6 %collective-permute-start.3 = (bf16[1056,256]{1,0:T(8,128)(2,1)}, bf16[1056,256]{1,0:T(8,128)(2,1)S(1)}, u32[]{:S(2)}, u32[]{:S(2)}) collective-permute-start(bf16[1056,256]{1,0:T(8,128)(2,1)} %get-tuple-element.56), channel_id=1, source_target_pairs={{0,3},{1,0},{2,1},{3,2},{4,7},{5,4},{6,5},{7,6},{8,11},{9,8},{10,9... | collective-permute-start | bytes 1622024 | tf_op jit(solution)/shard_map/ppermute | solution.py:383
  43.0 7.1 %first_partial.4 = (bf16[1056,256]{1,0:T(8,128)(2,1)}, bf16[1056,256]{1,0:T(8,128)(2,1)}, bf16[1056,1920]{1,0:T(8,128)(2,1)}) custom-call(s32[4]{0:T(128)} %get-tuple-element.98.shard_ref, bf16[1601,2,1920]{2,1,0:T(2,128)(2,1)} %bitcast.10, bf16[8,1920,256]{2,1,0:T(8,128)(2,1)} %split_heads.1.w_ref), custom_call_target="tpu_custom_call" | custom-call | flops 2076180480 | bytes 8110080 | tf_op jit(solution)/shard_map/first_partial/pallas_call | solution.py:70
  50.1 8.5 %later_partials.7 = (bf16[560,256]{1,0:T(8,128)(2,1)}, bf16[560,256]{1,0:T(8,128)(2,1)}, bf16[560,256]{1,0:T(8,128)(2,1)}, bf16[560,256]{1,0:T(8,128)(2,1)}, bf1...) custom-call(s32[4]{0:T(128)} %get-tuple-element.97.shard_ref, bf16[560,1920]{1,0:T(8,128)(2,1)} %get-tuple-element.68.flat_ref, ...), custom_call_target="tpu_custom_call" | custom-call | flops 3303014400 | bytes 2150400 | tf_op jit(solution)/shard_map/later_partials/pallas_call | solution.py:114
  58.6 12.7 %later_partials.5 = (bf16[1056,256]{1,0:T(8,128)(2,1)}, bf16[1056,256]{1,0:T(8,128)(2,1)}, bf16[1056,256]{1,0:T(8,128)(2,1)}, bf16[1056,256]{1,0:T(8,128)(2,1)},...) custom-call(s32[4]{0:T(128)} %get-tuple-element.97.shard_ref, bf16[1056,1920]{1,0:T(8,128)(2,1)} %get-tuple-element.57.flat_ref, ...), custom_call_target="tpu_custom_call" | custom-call | flops 6228541440 | bytes 4055040 | tf_op jit(solution)/shard_map/later_partials/pallas_call | solution.py:114
  71.3 12.7 %later_partials.4 = (bf16[1056,256]{1,0:T(8,128)(2,1)}, bf16[1056,256]{1,0:T(8,128)(2,1)}, bf16[1056,256]{1,0:T(8,128)(2,1)}, bf16[1056,256]{1,0:T(8,128)(2,1)},...) custom-call(s32[4]{0:T(128)} %get-tuple-element.98.shard_ref, bf16[1056,1920]{1,0:T(8,128)(2,1)} %get-tuple-element.52.flat_ref, ...), custom_call_target="tpu_custom_call" | custom-call | flops 6228541440 | bytes 4055040 | tf_op jit(solution)/shard_map/later_partials/pallas_call | solution.py:114
  84.1 8.6 %later_partials.6 = (bf16[560,256]{1,0:T(8,128)(2,1)}, bf16[560,256]{1,0:T(8,128)(2,1)}, bf16[560,256]{1,0:T(8,128)(2,1)}, bf16[560,256]{1,0:T(8,128)(2,1)}, bf1...) custom-call(s32[4]{0:T(128)} %get-tuple-element.98.shard_ref, bf16[560,1920]{1,0:T(8,128)(2,1)} %get-tuple-element.63.flat_ref, ...), custom_call_target="tpu_custom_call" | custom-call | flops 3303014400 | bytes 2150400 | tf_op jit(solution)/shard_map/later_partials/pallas_call | solution.py:114
  93.0 1.4 collective-permute-start
  94.7 2.7 %collective-permute-start.10 = (bf16[560,256]{1,0:T(8,128)(2,1)S(1)}, bf16[560,256]{1,0:T(8,128)(2,1)S(1)}, u32[]{:S(2)}, u32[]{:S(2)}) collective-permute-start(bf16[560,256]{1,0:T(8,128)(2,1)S(1)} %add_convert_fusion.13), channel_id=1, source_target_pairs={{0,3},{1,0},{2,1},{3,2},{4,7},{5,4},{6,5},{7,6},{8,11},{9,8},{10,9... | collective-permute-start | bytes 860168 | tf_op jit(solution)/shard_map/ppermute | solution.py:383
  97.5 7.0 %collective-permute-done.18 = bf16[1056,256]{1,0:T(8,128)(2,1)S(1)} collective-permute-done((bf16[1056,256]{1,0:T(8,128)(2,1)S(1)}, bf16[1056,256]{1,0:T(8,128)(2,1)S(1)}, u32[]{:S(2)}, u32[]{:S(2)}) %collective-permute-start.18) | collective-permute-done | bytes 540704 | tf_op jit(solution)/shard_map/ppermute | solution.py:383
  104.6 1.4 collective-permute-start.25
  107.2 10.1 %collective-permute-done.15 = bf16[1056,256]{1,0:T(8,128)(2,1)S(1)} collective-permute-done((bf16[1056,256]{1,0:T(8,128)(2,1)S(1)}, bf16[1056,256]{1,0:T(8,128)(2,1)S(1)}, u32[]{:S(2)}, u32[]{:S(2)}) %collective-permute-start.15) | collective-permute-done | bytes 540704 | tf_op jit(solution)/shard_map/ppermute | solution.py:383
  117.6 1.1 collective-permute-start.19
  119.3 0.8 add_convert_fusion.8
  120.1 3.5 %collective-permute-done.7 = bf16[560,256]{1,0:T(8,128)(2,1)S(1)} collective-permute-done((bf16[560,256]{1,0:T(8,128)(2,1)S(1)}, bf16[560,256]{1,0:T(8,128)(2,1)S(1)}, u32[]{:S(2)}, u32[]{:S(2)}) %collective-permute-start.7) | collective-permute-done | bytes 286752 | tf_op jit(solution)/shard_map/ppermute | solution.py:383
  123.7 2.2 collective-permute-done.4
  125.9 0.9 collective-permute-start.11
  127.0 9.7 %collective-permute-done.19 = bf16[1056,256]{1,0:T(8,128)(2,1)S(1)} collective-permute-done((bf16[1056,256]{1,0:T(8,128)(2,1)S(1)}, bf16[1056,256]{1,0:T(8,128)(2,1)S(1)}, u32[]{:S(2)}, u32[]{:S(2)}) %collective-permute-start.19) | collective-permute-done | bytes 540704 | tf_op jit(solution)/shard_map/ppermute | solution.py:383
  136.9 4.3 %collective-permute-done.1 = bf16[1056,256]{1,0:T(8,128)(2,1)S(1)} collective-permute-done((bf16[1056,256]{1,0:T(8,128)(2,1)S(1)}, bf16[1056,256]{1,0:T(8,128)(2,1)S(1)}, u32[]{:S(2)}, u32[]{:S(2)}) %collective-permute-start.1) | collective-permute-done | bytes 540704 | tf_op jit(solution)/shard_map/ppermute | solution.py:383
  141.4 11.4 %collective-permute-done.16 = bf16[1056,256]{1,0:T(8,128)(2,1)S(1)} collective-permute-done((bf16[1056,256]{1,0:T(8,128)(2,1)S(1)}, bf16[1056,256]{1,0:T(8,128)(2,1)S(1)}, u32[]{:S(2)}, u32[]{:S(2)}) %collective-permute-start.16) | collective-permute-done | bytes 540704 | tf_op jit(solution)/shard_map/ppermute | solution.py:383
  153.2 2.5 %collective-permute-start.20 = (bf16[1056,256]{1,0:T(8,128)(2,1)S(1)}, bf16[1056,256]{1,0:T(8,128)(2,1)S(1)}, u32[]{:S(2)}, u32[]{:S(2)}) collective-permute-start(bf16[1056,256]{1,0:T(8,128)(2,1)S(1)} %add_convert_fusion), channel_id=1, source_target_pairs={{0,3},{1,0},{2,1},{3,2},{4,7},{5,4},{6,5},{7,6},{8,11},{9,8},{10,9... | collective-permute-start | bytes 1622024 | tf_op jit(solution)/shard_map/ppermute | solution.py:383
  155.8 0.8 add_convert_fusion.10
  156.5 2.4 %collective-permute-done.8.up = bf16[560,256]{1,0:T(8,128)(2,1)S(1)} collective-permute-done((bf16[560,256]{1,0:T(8,128)(2,1)S(1)}, bf16[560,256]{1,0:T(8,128)(2,1)S(1)}, u32[]{:S(2)}, u32[]{:S(2)}) %collective-permute-start.8) | collective-permute-done | bytes 286752 | tf_op jit(solution)/shard_map/ppermute | solution.py:383
  159.7 0.8 collective-permute-start.23
  163.6 10.6 %all-reduce.1 = s32[1056]{0:T(1024)S(1)} all-reduce(s32[1056]{0:T(1024)S(1)} %dynamic-update-slice), channel_id=2, replica_groups={{0,4,8,12},{16,20,24,28},{32,36,40,44},{48,52,56,60},{64,68,72,76},{80,..., use_global_device_ids=true, to_apply=%add.1 | all-reduce | flops 1056 | bytes 8448
  174.4 0.8 reshape.7.mask_ref
  175.8 2.5 %prepare_queries.1 = (bf16[2,2,512,128]{3,2,1,0:T(8,128)(2,1)}, f32[4,2,64,128]{3,2,1,0:T(8,128)}) custom-call(s32[5,8]{1,0:T(8,128)} %concatenate.12.info_ref, s32[4,64,4]{2,1,0:T(8,128)} %reshape.7.mask_ref, bf16[4,64,2048]{2,1,0:T(8,128)(2,1)} %all-gather.3.cloned.1.call-done.q_ref, f32[1,128]{1,0:T(1,128)} %bitcast.17), custom_call_target="tpu_custom_call" | custom-call | flops 4194304 | bytes 2097152 | tf_op jit(solution)/shard_map/prepare_queries/pallas_call | solution.py:163
  178.3 3.9 %partial_attention.2.before_ref = f32[2,512,256]{2,1,0:T(8,128)} custom-call(bf16[560,256]{1,0:T(8,128)(2,1)} %copy-done.12, bf16[560,256]{1,0:T(8,128)(2,1)} %get-tuple-element.66.up_own, bf16[560,256]{1,0:T(8,128)(2,1)} %collective-permute-done.11.down, bf16[560,256]{1,0:T(8,128)(2,1)} %get-tuple-element.71.down_own, ...), custom_call_target="tpu_custom_call" | custom-call | flops 440401920 | bytes 1146880 | tf_op jit(solution)/shard_map/partial_attention/pallas_call | solution.py:212
  182.1 5.4 %closing_attention.2 = (f32[512,256]{1,0:T(8,128)}, bf16[528,128]{1,0:T(8,128)(2,1)}, bf16[528,128]{1,0:T(8,128)(2,1)}, bf16[528,128]{1,0:T(8,128)(2,1)}) custom-call(bf16[1056,256]{1,0:T(8,128)(2,1)} %collective-permute-done.2.up, bf16[1056,256]{1,0:T(8,128)(2,1)} %get-tuple-element.55.up_own, bf16[1056,256]{1,0:T(8,128)(2,1)} %copy-done.10, ...), custom_call_target="tpu_custom_call" | custom-call | flops 830472192 | bytes 2162688 | tf_op jit(solution)/shard_map/closing_attention/pallas_call | solution.py:274
  187.6 0.9 collective-permute-start.12
  188.6 3.9 %partial_attention.3.before_ref = f32[2,512,256]{2,1,0:T(8,128)} custom-call(bf16[560,256]{1,0:T(8,128)(2,1)} %collective-permute-done.23.up, bf16[560,256]{1,0:T(8,128)(2,1)} %get-tuple-element.88.up_own, bf16[560,256]{1,0:T(8,128)(2,1)} %collective-permute-done.26.down, bf16[560,256]{1,0:T(8,128)(2,1)} %get-tuple-element.92.down_own, ...), custom_call_target="tpu_custom_call" | custom-call | flops 440401920 | bytes 1146880 | tf_op jit(solution)/shard_map/partial_attention/pallas_call | solution.py:212
  192.5 1.0 collective-permute-start.13
  193.5 3.7 %collective-permute-start.14 = (bf16[528,128]{1,0:T(8,128)(2,1)S(1)}, bf16[528,128]{1,0:T(8,128)(2,1)S(1)}, u32[]{:S(2)}, u32[]{:S(2)}) collective-permute-start(bf16[528,128]{1,0:T(8,128)(2,1)S(1)} %copy-done.32), channel_id=1, source_target_pairs={{0,12},{4,8},{8,4},{12,0},{16,28},{20,24},{24,20},{28,16},{32,44},... | collective-permute-start | bytes 405512 | tf_op jit(solution)/shard_map/ppermute | solution.py:417
  197.2 0.8 copy-done.8
  198.2 5.5 %closing_attention.3 = (f32[512,256]{1,0:T(8,128)}, bf16[528,128]{1,0:T(8,128)(2,1)}, bf16[528,128]{1,0:T(8,128)(2,1)}, bf16[528,128]{1,0:T(8,128)(2,1)}) custom-call(bf16[1056,256]{1,0:T(8,128)(2,1)} %copy-done.9, bf16[1056,256]{1,0:T(8,128)(2,1)} %get-tuple-element.80.up_own, bf16[1056,256]{1,0:T(8,128)(2,1)} %copy-done.8, ...), custom_call_target="tpu_custom_call" | custom-call | flops 830472192 | bytes 2162688 | tf_op jit(solution)/shard_map/closing_attention/pallas_call | solution.py:274
  203.6 1.2 collective-permute-start.28
  204.9 0.9 collective-permute-start.29
  205.8 0.7 add_bitcast_fusion.info_ref
  206.5 2.1 collective-permute-done.28.refs_6_
  208.6 3.5 %collective-permute-done.29.refs_7_ = bf16[528,128]{1,0:T(8,128)(2,1)S(1)} collective-permute-done((bf16[528,128]{1,0:T(8,128)(2,1)}, bf16[528,128]{1,0:T(8,128)(2,1)S(1)}, u32[]{:S(2)}, u32[]{:S(2)}) %collective-permute-start.29) | collective-permute-done | bytes 135200 | tf_op jit(solution)/shard_map/ppermute | solution.py:417
  212.1 0.6 copy-done.26
  212.7 2.4 %finish.1 = bf16[1,64,2048]{2,1,0:T(8,128)(2,1)} custom-call(s32[1,8]{1,0:T(1,128)} %add_bitcast_fusion.info_ref, s32[1,64,4]{2,1,0:T(8,128)} %copy-done.11, f32[512,256]{1,0:T(8,128)} %get-tuple-element.73.refs_0_, bf16[528,128]{1,0:T(8,128)(2,1)} %copy-done.21, bf16[528,128]{1,0:T(8,128)(2,1)} %copy-done.22, bf16[528,128]{1,0:T(8,128)(2,1)} %copy-done.23, ...), custom_call_target="tpu_custom_call" | custom-call | flops 2097152 | bytes 2097152 | tf_op jit(solution)/shard_map/finish/pallas_call | solution.py:327
  (131 shorter events, 7.3 us)
Async XLA Ops:
  6.5 169.3 %all-gather.3.cloned.1.call-start = ((), (), s32[]{:S(2)}) async-start(), calls=%async_computation | async-start | bytes 1310720 | tf_op jit(solution)/shard_map/all_gather | solution.py:391
  21.3 71.7 %collective-permute-start.9 = (bf16[560,256]{1,0:T(8,128)(2,1)}, bf16[560,256]{1,0:T(8,128)(2,1)S(1)}, u32[]{:S(2)}, u32[]{:S(2)}) collective-permute-start(bf16[560,256]{1,0:T(8,128)(2,1)} %get-tuple-element.67), channel_id=1, source_target_pairs={{0,3},{1,0},{2,1},{3,2},{4,7},{5,4},{6,5},{7,6},{8,11},{9,8},{10,9... | collective-permute-start | bytes 860168 | tf_op jit(solution)/shard_map/ppermute | solution.py:383
  25.9 66.9 %collective-permute-start.24 = (bf16[560,256]{1,0:T(8,128)(2,1)}, bf16[560,256]{1,0:T(8,128)(2,1)S(1)}, u32[]{:S(2)}, u32[]{:S(2)}) collective-permute-start(bf16[560,256]{1,0:T(8,128)(2,1)} %get-tuple-element.89), channel_id=1, source_target_pairs={{0,3},{1,0},{2,1},{3,2},{4,7},{5,4},{6,5},{7,6},{8,11},{9,8},{10,9... | collective-permute-start | bytes 860168 | tf_op jit(solution)/shard_map/ppermute | solution.py:383
  31.9 62.8 %collective-permute-start.6 = (bf16[560,256]{1,0:T(8,128)(2,1)}, bf16[560,256]{1,0:T(8,128)(2,1)S(1)}, u32[]{:S(2)}, u32[]{:S(2)}) collective-permute-start(bf16[560,256]{1,0:T(8,128)(2,1)} %get-tuple-element.62), channel_id=1, source_target_pairs={{0,1},{1,2},{2,3},{3,0},{4,5},{5,6},{6,7},{7,4},{8,9},{9,10},{10,1... | collective-permute-start | bytes 860168 | tf_op jit(solution)/shard_map/ppermute | solution.py:383
  33.2 61.3 %collective-permute-start.21 = (bf16[560,256]{1,0:T(8,128)(2,1)}, bf16[560,256]{1,0:T(8,128)(2,1)S(1)}, u32[]{:S(2)}, u32[]{:S(2)}) collective-permute-start(bf16[560,256]{1,0:T(8,128)(2,1)} %get-tuple-element.85), channel_id=1, source_target_pairs={{0,1},{1,2},{2,3},{3,0},{4,5},{5,6},{6,7},{7,4},{8,9},{9,10},{10,1... | collective-permute-start | bytes 860168 | tf_op jit(solution)/shard_map/ppermute | solution.py:383
  40.3 65.7 %collective-permute-start.3 = (bf16[1056,256]{1,0:T(8,128)(2,1)}, bf16[1056,256]{1,0:T(8,128)(2,1)S(1)}, u32[]{:S(2)}, u32[]{:S(2)}) collective-permute-start(bf16[1056,256]{1,0:T(8,128)(2,1)} %get-tuple-element.56), channel_id=1, source_target_pairs={{0,3},{1,0},{2,1},{3,2},{4,7},{5,4},{6,5},{7,6},{8,11},{9,8},{10,9... | collective-permute-start | bytes 1622024 | tf_op jit(solution)/shard_map/ppermute | solution.py:383
  84.1 8.6 %copy-start.31 = (bf16[1056,256]{1,0:T(8,128)(2,1)S(1)}, bf16[1056,256]{1,0:T(8,128)(2,1)}, u32[]{:S(2)}) copy-start(bf16[1056,256]{1,0:T(8,128)(2,1)} %get-tuple-element.81) | copy-start | bytes 1622020
  84.1 8.9 %copy-start.19 = (bf16[560,256]{1,0:T(8,128)(2,1)S(1)}, bf16[560,256]{1,0:T(8,128)(2,1)}, u32[]{:S(2)}) copy-start(bf16[560,256]{1,0:T(8,128)(2,1)} %get-tuple-element.90) | copy-start | bytes 860164
  84.1 8.9 %copy-start.30 = (bf16[1056,256]{1,0:T(8,128)(2,1)S(1)}, bf16[1056,256]{1,0:T(8,128)(2,1)}, u32[]{:S(2)}) copy-start(bf16[1056,256]{1,0:T(8,128)(2,1)} %get-tuple-element.51) | copy-start | bytes 1622020
  84.1 10.4 %copy-start.17 = (bf16[560,256]{1,0:T(8,128)(2,1)S(1)}, bf16[560,256]{1,0:T(8,128)(2,1)}, u32[]{:S(2)}) copy-start(bf16[560,256]{1,0:T(8,128)(2,1)} %get-tuple-element.69) | copy-start | bytes 860164
  92.7 11.8 %collective-permute-start.18 = (bf16[1056,256]{1,0:T(8,128)(2,1)S(1)}, bf16[1056,256]{1,0:T(8,128)(2,1)S(1)}, u32[]{:S(2)}, u32[]{:S(2)}) collective-permute-start(bf16[1056,256]{1,0:T(8,128)(2,1)S(1)} %copy-done.31), channel_id=1, source_target_pairs={{0,3},{1,0},{2,1},{3,2},{4,7},{5,4},{6,5},{7,6},{8,11},{9,8},{10,9... | collective-permute-start | bytes 1622024 | tf_op jit(solution)/shard_map/ppermute | solution.py:383
  93.0 13.4 %collective-permute-start = (bf16[1056,256]{1,0:T(8,128)(2,1)S(1)}, bf16[1056,256]{1,0:T(8,128)(2,1)S(1)}, u32[]{:S(2)}, u32[]{:S(2)}) collective-permute-start(bf16[1056,256]{1,0:T(8,128)(2,1)S(1)} %copy-done.30), channel_id=1, source_target_pairs={{0,1},{1,2},{2,3},{3,0},{4,5},{5,6},{6,7},{7,4},{8,9},{9,10},{10,1... | collective-permute-start | bytes 1622024 | tf_op jit(solution)/shard_map/ppermute | solution.py:383
  94.4 11.5 %copy-start.7 = (bf16[1056,256]{1,0:T(8,128)(2,1)S(1)}, bf16[1056,256]{1,0:T(8,128)(2,1)}, u32[]{:S(2)}) copy-start(bf16[1056,256]{1,0:T(8,128)(2,1)} %get-tuple-element.82) | copy-start | bytes 1622020
  94.6 22.8 %collective-permute-start.15 = (bf16[1056,256]{1,0:T(8,128)(2,1)S(1)}, bf16[1056,256]{1,0:T(8,128)(2,1)S(1)}, u32[]{:S(2)}, u32[]{:S(2)}) collective-permute-start(bf16[1056,256]{1,0:T(8,128)(2,1)S(1)} %copy-done.29), channel_id=1, source_target_pairs={{0,1},{1,2},{2,3},{3,0},{4,5},{5,6},{6,7},{7,4},{8,9},{9,10},{10,1... | collective-permute-start | bytes 1622024 | tf_op jit(solution)/shard_map/ppermute | solution.py:383
  94.7 22.8 %collective-permute-start.10 = (bf16[560,256]{1,0:T(8,128)(2,1)S(1)}, bf16[560,256]{1,0:T(8,128)(2,1)S(1)}, u32[]{:S(2)}, u32[]{:S(2)}) collective-permute-start(bf16[560,256]{1,0:T(8,128)(2,1)S(1)} %add_convert_fusion.13), channel_id=1, source_target_pairs={{0,3},{1,0},{2,1},{3,2},{4,7},{5,4},{6,5},{7,6},{8,11},{9,8},{10,9... | collective-permute-start | bytes 860168 | tf_op jit(solution)/shard_map/ppermute | solution.py:383
  97.5 8.8 %copy-start.6 = (bf16[1056,256]{1,0:T(8,128)(2,1)S(1)}, bf16[1056,256]{1,0:T(8,128)(2,1)}, u32[]{:S(2)}) copy-start(bf16[1056,256]{1,0:T(8,128)(2,1)} %get-tuple-element.58) | copy-start | bytes 1622020
  104.6 14.2 %collective-permute-start.25 = (bf16[560,256]{1,0:T(8,128)(2,1)S(1)}, bf16[560,256]{1,0:T(8,128)(2,1)S(1)}, u32[]{:S(2)}, u32[]{:S(2)}) collective-permute-start(bf16[560,256]{1,0:T(8,128)(2,1)S(1)} %add_convert_fusion.9), channel_id=1, source_target_pairs={{0,3},{1,0},{2,1},{3,2},{4,7},{5,4},{6,5},{7,6},{8,11},{9,8},{10,9... | collective-permute-start | bytes 860168 | tf_op jit(solution)/shard_map/ppermute | solution.py:383
  106.1 17.5 %collective-permute-start.7 = (bf16[560,256]{1,0:T(8,128)(2,1)S(1)}, bf16[560,256]{1,0:T(8,128)(2,1)S(1)}, u32[]{:S(2)}, u32[]{:S(2)}) collective-permute-start(bf16[560,256]{1,0:T(8,128)(2,1)S(1)} %add_convert_fusion.15), channel_id=1, source_target_pairs={{0,1},{1,2},{2,3},{3,0},{4,5},{5,6},{6,7},{7,4},{8,9},{9,10},{10,1... | collective-permute-start | bytes 860168 | tf_op jit(solution)/shard_map/ppermute | solution.py:383
  106.4 11.0 %copy-start.4 = (bf16[1056,256]{1,0:T(8,128)(2,1)S(1)}, bf16[1056,256]{1,0:T(8,128)(2,1)}, u32[]{:S(2)}) copy-start(bf16[1056,256]{1,0:T(8,128)(2,1)} %get-tuple-element.78) | copy-start | bytes 1622020
  106.4 46.8 %collective-permute-start.22 = (bf16[560,256]{1,0:T(8,128)(2,1)S(1)}, bf16[560,256]{1,0:T(8,128)(2,1)S(1)}, u32[]{:S(2)}, u32[]{:S(2)}) collective-permute-start(bf16[560,256]{1,0:T(8,128)(2,1)S(1)} %add_convert_fusion.11), channel_id=1, source_target_pairs={{0,1},{1,2},{2,3},{3,0},{4,5},{5,6},{6,7},{7,4},{8,9},{9,10},{10,1... | collective-permute-start | bytes 860168 | tf_op jit(solution)/shard_map/ppermute | solution.py:383
  107.2 11.4 %copy-start.15 = (bf16[560,256]{1,0:T(8,128)(2,1)S(1)}, bf16[560,256]{1,0:T(8,128)(2,1)}, u32[]{:S(2)}) copy-start(bf16[560,256]{1,0:T(8,128)(2,1)} %get-tuple-element.70) | copy-start | bytes 860164
  117.4 8.5 %collective-permute-start.4 = (bf16[1056,256]{1,0:T(8,128)(2,1)S(1)}, bf16[1056,256]{1,0:T(8,128)(2,1)S(1)}, u32[]{:S(2)}, u32[]{:S(2)}) collective-permute-start(bf16[1056,256]{1,0:T(8,128)(2,1)S(1)} %add_convert_fusion.5), channel_id=1, source_target_pairs={{0,3},{1,0},{2,1},{3,2},{4,7},{5,4},{6,5},{7,6},{8,11},{9,8},{10,9... | collective-permute-start | bytes 1622024 | tf_op jit(solution)/shard_map/ppermute | solution.py:383
  117.6 19.1 %collective-permute-start.19 = (bf16[1056,256]{1,0:T(8,128)(2,1)S(1)}, bf16[1056,256]{1,0:T(8,128)(2,1)S(1)}, u32[]{:S(2)}, u32[]{:S(2)}) collective-permute-start(bf16[1056,256]{1,0:T(8,128)(2,1)S(1)} %add_convert_fusion.1), channel_id=1, source_target_pairs={{0,3},{1,0},{2,1},{3,2},{4,7},{5,4},{6,5},{7,6},{8,11},{9,8},{10,9... | collective-permute-start | bytes 1622024 | tf_op jit(solution)/shard_map/ppermute | solution.py:383
  118.7 22.5 %collective-permute-start.1 = (bf16[1056,256]{1,0:T(8,128)(2,1)S(1)}, bf16[1056,256]{1,0:T(8,128)(2,1)S(1)}, u32[]{:S(2)}, u32[]{:S(2)}) collective-permute-start(bf16[1056,256]{1,0:T(8,128)(2,1)S(1)} %add_convert_fusion.7), channel_id=1, source_target_pairs={{0,1},{1,2},{2,3},{3,0},{4,5},{5,6},{6,7},{7,4},{8,9},{9,10},{10,1... | collective-permute-start | bytes 1622024 | tf_op jit(solution)/shard_map/ppermute | solution.py:383
  123.5 29.3 %collective-permute-start.16 = (bf16[1056,256]{1,0:T(8,128)(2,1)S(1)}, bf16[1056,256]{1,0:T(8,128)(2,1)S(1)}, u32[]{:S(2)}, u32[]{:S(2)}) collective-permute-start(bf16[1056,256]{1,0:T(8,128)(2,1)S(1)} %add_convert_fusion.3), channel_id=1, source_target_pairs={{0,1},{1,2},{2,3},{3,0},{4,5},{5,6},{6,7},{7,4},{8,9},{9,10},{10,1... | collective-permute-start | bytes 1622024 | tf_op jit(solution)/shard_map/ppermute | solution.py:383
  123.6 13.1 %copy-start.2 = (bf16[1056,256]{1,0:T(8,128)(2,1)S(1)}, bf16[1056,256]{1,0:T(8,128)(2,1)}, u32[]{:S(2)}) copy-start(bf16[1056,256]{1,0:T(8,128)(2,1)} %get-tuple-element.83) | copy-start | bytes 1622020
  125.9 29.9 %collective-permute-start.11 = (bf16[560,256]{1,0:T(8,128)(2,1)S(1)}, bf16[560,256]{1,0:T(8,128)(2,1)}, u32[]{:S(2)}, u32[]{:S(2)}) collective-permute-start(bf16[560,256]{1,0:T(8,128)(2,1)S(1)} %add_convert_fusion.12), channel_id=1, source_target_pairs={{0,3},{1,0},{2,1},{3,2},{4,7},{5,4},{6,5},{7,6},{8,11},{9,8},{10,9... | collective-permute-start | bytes 860168 | tf_op jit(solution)/shard_map/ppermute | solution.py:383
  126.9 14.3 %copy-start.1 = (bf16[1056,256]{1,0:T(8,128)(2,1)S(1)}, bf16[1056,256]{1,0:T(8,128)(2,1)}, u32[]{:S(2)}) copy-start(bf16[1056,256]{1,0:T(8,128)(2,1)} %get-tuple-element.54) | copy-start | bytes 1622020
  136.7 22.3 %collective-permute-start.8 = (bf16[560,256]{1,0:T(8,128)(2,1)S(1)}, bf16[560,256]{1,0:T(8,128)(2,1)S(1)}, u32[]{:S(2)}, u32[]{:S(2)}) collective-permute-start(bf16[560,256]{1,0:T(8,128)(2,1)S(1)} %add_convert_fusion.14), channel_id=1, source_target_pairs={{0,1},{1,2},{2,3},{3,0},{4,5},{5,6},{6,7},{7,4},{8,9},{9,10},{10,1... | collective-permute-start | bytes 860168 | tf_op jit(solution)/shard_map/ppermute | solution.py:383
  136.9 16.1 %copy-start = (bf16[1056,256]{1,0:T(8,128)(2,1)S(1)}, bf16[1056,256]{1,0:T(8,128)(2,1)}, u32[]{:S(2)}) copy-start(bf16[1056,256]{1,0:T(8,128)(2,1)} %get-tuple-element.79) | copy-start | bytes 1622020
  141.3 18.0 %collective-permute-start.5 = (bf16[1056,256]{1,0:T(8,128)(2,1)S(1)}, bf16[1056,256]{1,0:T(8,128)(2,1)S(1)}, u32[]{:S(2)}, u32[]{:S(2)}) collective-permute-start(bf16[1056,256]{1,0:T(8,128)(2,1)S(1)} %add_convert_fusion.4), channel_id=1, source_target_pairs={{0,3},{1,0},{2,1},{3,2},{4,7},{5,4},{6,5},{7,6},{8,11},{9,8},{10,9... | collective-permute-start | bytes 1622024 | tf_op jit(solution)/shard_map/ppermute | solution.py:383
  141.4 14.4 %copy-start.13 = (bf16[560,256]{1,0:T(8,128)(2,1)S(1)}, bf16[560,256]{1,0:T(8,128)(2,1)}, u32[]{:S(2)}) copy-start(bf16[560,256]{1,0:T(8,128)(2,1)} %get-tuple-element.87) | copy-start | bytes 860164
  152.8 29.3 %collective-permute-start.2 = (bf16[1056,256]{1,0:T(8,128)(2,1)S(1)}, bf16[1056,256]{1,0:T(8,128)(2,1)}, u32[]{:S(2)}, u32[]{:S(2)}) collective-permute-start(bf16[1056,256]{1,0:T(8,128)(2,1)S(1)} %add_convert_fusion.6), channel_id=1, source_target_pairs={{0,1},{1,2},{2,3},{3,0},{4,5},{5,6},{6,7},{7,4},{8,9},{9,10},{10,1... | collective-permute-start | bytes 1622024 | tf_op jit(solution)/shard_map/ppermute | solution.py:383
  153.1 8.8 %copy-start.27 = (s32[1,64,4]{1,2,0:T(4,128)S(1)}, s32[1,64,4]{1,2,0:T(4,128)}, u32[]{:S(2)}) copy-start(s32[1,64,4]{1,2,0:T(4,128)} %param.16) | copy-start | bytes 3076
  153.1 9.0 %copy-start.34 = (u32[128]{0:T(128)S(1)}, u32[128]{0:T(128)}, u32[]{:S(2)}) copy-start(u32[128]{0:T(128)} %constant.31) | copy-start | bytes 1540
  153.1 10.2 %copy-start.28 = (s32[1,4]{1,0:T(1,128)S(1)}, s32[1,4]{1,0:T(1,128)}, u32[]{:S(2)}) copy-start(s32[1,4]{1,0:T(1,128)} %param.15) | copy-start | bytes 52
  153.2 44.0 %collective-permute-start.20 = (bf16[1056,256]{1,0:T(8,128)(2,1)S(1)}, bf16[1056,256]{1,0:T(8,128)(2,1)S(1)}, u32[]{:S(2)}, u32[]{:S(2)}) collective-permute-start(bf16[1056,256]{1,0:T(8,128)(2,1)S(1)} %add_convert_fusion), channel_id=1, source_target_pairs={{0,3},{1,0},{2,1},{3,2},{4,7},{5,4},{6,5},{7,6},{8,11},{9,8},{10,9... | collective-permute-start | bytes 1622024 | tf_op jit(solution)/shard_map/ppermute | solution.py:383
  155.8 41.4 %collective-permute-start.17 = (bf16[1056,256]{1,0:T(8,128)(2,1)S(1)}, bf16[1056,256]{1,0:T(8,128)(2,1)S(1)}, u32[]{:S(2)}, u32[]{:S(2)}) collective-permute-start(bf16[1056,256]{1,0:T(8,128)(2,1)S(1)} %add_convert_fusion.2), channel_id=1, source_target_pairs={{0,1},{1,2},{2,3},{3,0},{4,5},{5,6},{6,7},{7,4},{8,9},{9,10},{10,1... | collective-permute-start | bytes 1622024 | tf_op jit(solution)/shard_map/ppermute | solution.py:383
  159.0 29.5 %collective-permute-start.26 = (bf16[560,256]{1,0:T(8,128)(2,1)}, bf16[560,256]{1,0:T(8,128)(2,1)}, u32[]{:S(2)}, u32[]{:S(2)}) collective-permute-start(bf16[560,256]{1,0:T(8,128)(2,1)} %add_convert_fusion.8), channel_id=1, source_target_pairs={{0,3},{1,0},{2,1},{3,2},{4,7},{5,4},{6,5},{7,6},{8,11},{9,8},{10,9... | collective-permute-start | bytes 860168 | tf_op jit(solution)/shard_map/ppermute | solution.py:383
  159.7 22.4 %copy-start.10 = (bf16[1056,256]{1,0:T(8,128)(2,1)}, bf16[1056,256]{1,0:T(8,128)(2,1)S(1)}, u32[]{:S(2)}) copy-start(bf16[1056,256]{1,0:T(8,128)(2,1)S(1)} %collective-permute-done.5.down) | copy-start | bytes 1622020
  159.7 28.8 %collective-permute-start.23 = (bf16[560,256]{1,0:T(8,128)(2,1)}, bf16[560,256]{1,0:T(8,128)(2,1)}, u32[]{:S(2)}, u32[]{:S(2)}) collective-permute-start(bf16[560,256]{1,0:T(8,128)(2,1)} %add_convert_fusion.10), channel_id=1, source_target_pairs={{0,1},{1,2},{2,3},{3,0},{4,5},{5,6},{6,7},{7,4},{8,9},{9,10},{10,1... | collective-permute-start | bytes 860168 | tf_op jit(solution)/shard_map/ppermute | solution.py:383
  161.9 20.2 %copy-start.11 = (s32[1,64,4]{2,1,0:T(8,128)}, s32[1,64,4]{2,1,0:T(8,128)S(1)}, u32[]{:S(2)}) copy-start(s32[1,64,4]{2,1,0:T(8,128)S(1)} %copy.14.mask_ref) | copy-start | bytes 3076
  187.6 17.3 %collective-permute-start.12 = (bf16[528,128]{1,0:T(8,128)(2,1)}, bf16[528,128]{1,0:T(8,128)(2,1)S(1)}, u32[]{:S(2)}, u32[]{:S(2)}) collective-permute-start(bf16[528,128]{1,0:T(8,128)(2,1)} %get-tuple-element.74), channel_id=1, source_target_pairs={{0,4},{4,0},{8,12},{12,8},{16,20},{20,16},{24,28},{28,24},{32,36},... | collective-permute-start | bytes 405512 | tf_op jit(solution)/shard_map/ppermute | solution.py:417
  192.5 14.0 %collective-permute-start.13 = (bf16[528,128]{1,0:T(8,128)(2,1)S(1)}, bf16[528,128]{1,0:T(8,128)(2,1)S(1)}, u32[]{:S(2)}, u32[]{:S(2)}) collective-permute-start(bf16[528,128]{1,0:T(8,128)(2,1)S(1)} %copy-done.33), channel_id=1, source_target_pairs={{0,8},{4,12},{8,0},{12,4},{16,24},{20,28},{24,16},{28,20},{32,40},... | collective-permute-start | bytes 405512 | tf_op jit(solution)/shard_map/ppermute | solution.py:417
  193.5 12.9 %collective-permute-start.14 = (bf16[528,128]{1,0:T(8,128)(2,1)S(1)}, bf16[528,128]{1,0:T(8,128)(2,1)S(1)}, u32[]{:S(2)}, u32[]{:S(2)}) collective-permute-start(bf16[528,128]{1,0:T(8,128)(2,1)S(1)} %copy-done.32), channel_id=1, source_target_pairs={{0,12},{4,8},{8,4},{12,0},{16,28},{20,24},{24,20},{28,16},{32,44},... | collective-permute-start | bytes 405512 | tf_op jit(solution)/shard_map/ppermute | solution.py:417
  203.6 2.8 %collective-permute-start.27 = (bf16[528,128]{1,0:T(8,128)(2,1)}, bf16[528,128]{1,0:T(8,128)(2,1)S(1)}, u32[]{:S(2)}, u32[]{:S(2)}) collective-permute-start(bf16[528,128]{1,0:T(8,128)(2,1)} %get-tuple-element.94), channel_id=1, source_target_pairs={{0,4},{4,0},{8,12},{12,8},{16,20},{20,16},{24,28},{28,24},{32,36},... | collective-permute-start | bytes 405512 | tf_op jit(solution)/shard_map/ppermute | solution.py:417
  203.6 4.9 %collective-permute-start.28 = (bf16[528,128]{1,0:T(8,128)(2,1)}, bf16[528,128]{1,0:T(8,128)(2,1)S(1)}, u32[]{:S(2)}, u32[]{:S(2)}) collective-permute-start(bf16[528,128]{1,0:T(8,128)(2,1)} %get-tuple-element.95), channel_id=1, source_target_pairs={{0,8},{4,12},{8,0},{12,4},{16,24},{20,28},{24,16},{28,20},{32,40},... | collective-permute-start | bytes 405512 | tf_op jit(solution)/shard_map/ppermute | solution.py:417
  204.9 7.2 %collective-permute-start.29 = (bf16[528,128]{1,0:T(8,128)(2,1)}, bf16[528,128]{1,0:T(8,128)(2,1)S(1)}, u32[]{:S(2)}, u32[]{:S(2)}) collective-permute-start(bf16[528,128]{1,0:T(8,128)(2,1)} %get-tuple-element.96), channel_id=1, source_target_pairs={{0,12},{4,8},{8,4},{12,0},{16,28},{20,24},{24,20},{28,16},{32,44},... | collective-permute-start | bytes 405512 | tf_op jit(solution)/shard_map/ppermute | solution.py:417
  (18 other events, 65.2 us)
Sparse Core Ops, SparseCore 0:
  9.0 24.4 all-gather.2
